TPU v7x, 32 devices: a whole 2x2x4 slice. The times are simulated.
32 devices in a mesh: ctx: 16 (over z, y, x), fsdp: 2 (over core).
Axes of the slice: x: 2, y: 2, z: 4, core: 2. Of those that a mesh axis runs over, the one named last changes fastest.
Arguments:
- layer_input: bfloat16 [2, 4096, 896], P('fsdp', 'ctx'), may hold values from -6 to 6
- out_cotangent: bfloat16 [2, 4096, 896], P('fsdp', 'ctx'), may hold values from -6 to 6
- span_perm: int32 [16], replicated, may hold values from 0 to 15, each once
- attn_gain: bfloat16 [896], P('fsdp'), may hold values from 0.25 to 1.75
- query_weight: bfloat16 [896, 896], P('fsdp'), may hold values from -0.25 to 0.25
- query_bias: bfloat16 [896], P('fsdp'), may hold values from -3 to 3
- key_weight: bfloat16 [896, 128], P('fsdp'), may hold values from -0.25 to 0.25
- key_bias: bfloat16 [128], P('fsdp'), may hold values from -3 to 3
- value_weight: bfloat16 [896, 128], P('fsdp'), may hold values from -0.1875 to 0.1875
- value_bias: bfloat16 [128], P('fsdp'), may hold values from -0.29882812 to 0.29882812
- output_weight: bfloat16 [896, 896], P('fsdp'), may hold values from -2 to 2
- mlp_gain: bfloat16 [896], P('fsdp'), may hold values from 0.25 to 1.75
- gate_weight: bfloat16 [896, 4864], P('fsdp'), may hold values from -0.1875 to 0.1875
- up_weight: bfloat16 [896, 4864], P('fsdp'), may hold values from -0.1875 to 0.1875
- down_weight: bfloat16 [4864, 896], P('fsdp'), may hold values from -0.078125 to 0.078125
Outputs:
- layer_output: bfloat16 [2, 4096, 896], P('fsdp', 'ctx')
- input_grad: float32 [2, 4096, 896], P('fsdp', 'ctx')
- attn_gain_grad: float32 [896], P('fsdp')
- query_weight_grad: float32 [896, 896], P('fsdp')
- query_bias_grad: float32 [896], P('fsdp')
- key_weight_grad: float32 [896, 128], P('fsdp')
- key_bias_grad: float32 [128], P('fsdp')
- value_weight_grad: float32 [896, 128], P('fsdp')
- value_bias_grad: float32 [128], P('fsdp')
- output_weight_grad: float32 [896, 896], P('fsdp')
- mlp_gain_grad: float32 [896], P('fsdp')
- gate_weight_grad: float32 [896, 4864], P('fsdp')
- up_weight_grad: float32 [896, 4864], P('fsdp')
- down_weight_grad: float32 [4864, 896], P('fsdp')
Inputs may be any that keep to these rules, and one draw needn't show every extreme that they name: span_perm is a permutation; index d of ctx holds span span_perm[d] of 128 tokens and then span 2 * 16 - 1 - span_perm[d].
All inputs are finite; a program needn't handle non-finite values.
Results may differ from a plain program's by a relative error of at most 0.028.
Values may be sent and summed in bfloat16 or wider, within the bound.
A program may use at most 256 MiB of HBM per device.

v0:
```python
import math

import jax
import jax.numpy as jnp
from jax import lax
from jax.sharding import PartitionSpec as P

HEADS = 14
KV_HEADS = 2
HEAD_DIM = 64


EPSILON = 1e-06
THETA_LOG = math.log(1000000.0)
NEGATIVE = -1e30


def cut_along(array, dim, peers):
    shape = array.shape
    blocks = array.reshape(*shape[:dim], peers, shape[dim] // peers, *shape[dim + 1 :])
    return jnp.moveaxis(blocks, dim, 0)


def summed_on_arrival(array, axis, dim):
    peers = lax.axis_size(axis)
    blocks = lax.all_to_all(cut_along(array, dim, peers), axis, 0, 0, tiled=True)
    return jnp.sum(blocks.astype(jnp.float32), axis=0)


def rms_scale(values, gain_vec):
    return (
        values * lax.rsqrt(jnp.mean(values * values, axis=-1, keepdims=True) + EPSILON) * gain_vec
    )


def swiglu(gate_act, up_act):
    return jax.nn.silu(gate_act) * up_act


def angle_table(places, head_size):
    half_dim = head_size // 2
    frequency = jnp.exp(-(2.0 * jnp.arange(half_dim, dtype=jnp.float32) / head_size) * THETA_LOG)
    return places.astype(jnp.float32)[:, None] * frequency[None, :]


def rotate(values, angles):
    half_dim = values.shape[-1] // 2
    cosine = jnp.cos(angles)[:, None, :]
    sine_part = jnp.sin(angles)[:, None, :]
    first_half = values[..., :half_dim]
    second = values[..., half_dim:]
    return jnp.concatenate(
        [first_half * cosine - second * sine_part, second * cosine + first_half * sine_part],
        axis=-1,
    )


def place_table(span_perm, tok_rows, ctx_count):
    row_ids = jnp.arange(tok_rows * ctx_count, dtype=jnp.int32)
    owner_dev = row_ids // tok_rows
    within = row_ids % tok_rows
    matches = owner_dev[:, None] == jnp.arange(ctx_count, dtype=jnp.int32)[None, :]
    first_span = jnp.sum(jnp.where(matches, span_perm[None, :], 0), axis=1)
    half_rows = tok_rows // 2
    span_id = jnp.where(within < half_rows, first_span, 2 * ctx_count - 1 - first_span)
    return span_id * half_rows + within % half_rows


def body(
    layer_input,
    out_cotangent,
    span_perm,
    attn_gain,
    query_weight,
    query_bias,
    key_weight,
    key_bias,
    value_weight,
    value_bias,
    output_weight,
    mlp_gain,
    gate_weight,
    up_weight,
    down_weight,
):
    f32 = jnp.float32
    bf16 = jnp.bfloat16
    tok_rows = layer_input.shape[1]
    ctx_count = lax.axis_size("ctx")
    ctx_index = lax.axis_index("ctx")
    group_size = HEADS // KV_HEADS
    kv_width = KV_HEADS * HEAD_DIM
    q_width = HEADS * HEAD_DIM
    score_scale = 1.0 / math.sqrt(HEAD_DIM)
    place_all = place_table(span_perm, tok_rows, ctx_count)
    place_mine = lax.dynamic_slice_in_dim(place_all, ctx_index * tok_rows, tok_rows)
    angles = angle_table(place_mine, HEAD_DIM)
    (
        gain_one,
        weight_query,
        bias_query,
        weight_key,
        bias_key,
        weight_value,
        bias_value,
        weight_out,
    ) = (
        lax.all_gather(attn_gain, "fsdp", axis=0, tiled=True),
        lax.all_gather(query_weight, "fsdp", axis=0, tiled=True),
        lax.all_gather(query_bias, "fsdp", axis=0, tiled=True),
        lax.all_gather(key_weight, "fsdp", axis=0, tiled=True),
        lax.all_gather(key_bias, "fsdp", axis=0, tiled=True),
        lax.all_gather(value_weight, "fsdp", axis=0, tiled=True),
        lax.all_gather(value_bias, "fsdp", axis=0, tiled=True),
        lax.all_gather(output_weight, "fsdp", axis=0, tiled=True),
    )
    inputs = layer_input[0].astype(f32)
    normed = rms_scale(inputs, gain_one.astype(f32)).astype(bf16)
    queries = jnp.dot(normed, weight_query, preferred_element_type=f32) + bias_query.astype(f32)
    key_proj = jnp.dot(normed, weight_key, preferred_element_type=f32) + bias_key.astype(f32)
    value_proj = jnp.dot(normed, weight_value, preferred_element_type=f32) + bias_value.astype(f32)
    query_rot = rotate(queries.reshape(tok_rows, HEADS, HEAD_DIM), angles).astype(bf16)
    query_rot = query_rot.reshape(tok_rows, KV_HEADS, group_size, HEAD_DIM)
    key_rot = rotate(key_proj.reshape(tok_rows, KV_HEADS, HEAD_DIM), angles).astype(bf16)
    kv_local = jnp.concatenate(
        [key_rot.reshape(tok_rows, kv_width), value_proj.astype(bf16)], axis=1
    )

    def split_piece(shard_rows):
        piece_rows = shard_rows.shape[0]
        block_rows = math.gcd(piece_rows, 512)
        key_blocks = shard_rows[:, :kv_width].reshape(
            piece_rows // block_rows, block_rows, KV_HEADS, HEAD_DIM
        )
        value_blocks = shard_rows[:, kv_width:].reshape(
            piece_rows // block_rows, block_rows, KV_HEADS, HEAD_DIM
        )
        key_places = place_all.reshape(piece_rows // block_rows, block_rows)
        return (piece_rows, block_rows, (key_blocks, value_blocks, key_places))

    start_state = (
        jnp.full((KV_HEADS, group_size, tok_rows), NEGATIVE, f32),
        jnp.zeros((KV_HEADS, group_size, tok_rows), f32),
        jnp.zeros((KV_HEADS, group_size, tok_rows, HEAD_DIM), f32),
    )
    carried = start_state
    piece_rows, block_rows, blocks = split_piece(
        lax.all_gather(kv_local, "ctx", axis=0, tiled=True)
    )

    def attend_block(inner, block_data):
        run_max, run_sum, run_out = inner
        key_block, value_block, key_place = block_data
        raw_scores = jnp.einsum("qhgd,khd->hgqk", query_rot, key_block, preferred_element_type=f32)
        allowed = place_mine[:, None] >= key_place[None, :]
        scores = jnp.where(allowed, score_scale * raw_scores, NEGATIVE)
        new_max = jnp.maximum(run_max, jnp.max(scores, axis=-1))
        factor = jnp.exp(run_max - new_max)
        weights = jnp.where(allowed, jnp.exp(scores - new_max[..., None]), 0.0)
        run_sum = factor * run_sum + jnp.sum(weights, axis=-1)
        run_out = factor[..., None] * run_out + jnp.einsum(
            "hgqk,khd->hgqd", weights.astype(bf16), value_block, preferred_element_type=f32
        )
        return ((new_max, run_sum, run_out), None)

    carried, _ = lax.scan(attend_block, carried, blocks)
    run_max, run_sum, run_out = carried
    attn_heads = run_out / run_sum[..., None]
    log_total = run_max + jnp.log(run_sum)
    mixed = jnp.transpose(attn_heads, (2, 0, 1, 3)).reshape(tok_rows, q_width).astype(bf16)
    middle = inputs + jnp.dot(mixed, weight_out, preferred_element_type=f32)
    gain_two, weight_gate, weight_up, weight_down = (
        lax.all_gather(mlp_gain, "fsdp", axis=0, tiled=True),
        lax.all_gather(gate_weight, "fsdp", axis=0, tiled=True),
        lax.all_gather(up_weight, "fsdp", axis=0, tiled=True),
        lax.all_gather(down_weight, "fsdp", axis=0, tiled=True),
    )
    normed_two = rms_scale(middle, gain_two.astype(f32)).astype(bf16)
    gate_act = jnp.dot(normed_two, weight_gate, preferred_element_type=f32)
    up_act = jnp.dot(normed_two, weight_up, preferred_element_type=f32)
    hidden = swiglu(gate_act, up_act).astype(bf16)
    layer_output = (middle + jnp.dot(hidden, weight_down, preferred_element_type=f32)).astype(bf16)
    out_grad = out_cotangent[0]
    grad_down = jnp.einsum("tf,td->fd", hidden, out_grad, preferred_element_type=f32)
    grad_hidden = jnp.einsum("td,fd->tf", out_grad, weight_down, preferred_element_type=f32)
    grad_gate, grad_up = jax.vjp(swiglu, gate_act, up_act)[1](grad_hidden)
    grad_gate = grad_gate.astype(bf16)
    grad_up = grad_up.astype(bf16)
    grad_wgate = jnp.einsum("td,tf->df", normed_two, grad_gate, preferred_element_type=f32)
    grad_wup = jnp.einsum("td,tf->df", normed_two, grad_up, preferred_element_type=f32)
    grad_normed_two = jnp.einsum(
        "tf,df->td", grad_gate, weight_gate, preferred_element_type=f32
    ) + jnp.einsum("tf,df->td", grad_up, weight_up, preferred_element_type=f32)
    grad_middle_part, grad_gain_two = jax.vjp(rms_scale, middle, gain_two.astype(f32))[1](
        grad_normed_two
    )
    grad_middle = out_grad.astype(f32) + grad_middle_part
    grad_branch = grad_middle.astype(bf16)
    grad_wout = jnp.einsum("tq,td->qd", mixed, grad_branch, preferred_element_type=f32)
    grad_mixed = jnp.einsum(
        "td,qd->tq", grad_branch, weight_out, preferred_element_type=f32
    ).astype(bf16)
    grad_heads = jnp.transpose(
        grad_mixed.reshape(tok_rows, KV_HEADS, group_size, HEAD_DIM), (1, 2, 0, 3)
    )
    delta = jnp.sum(grad_heads.astype(f32) * attn_heads, axis=-1)
    grad_query_acc = jnp.zeros((KV_HEADS, group_size, tok_rows, HEAD_DIM), f32)
    piece_rows, block_rows, blocks = split_piece(
        lax.all_gather(kv_local, "ctx", axis=0, tiled=True)
    )

    def attend_back(grad_query, block_data):
        key_block, value_block, key_place = block_data
        raw_scores = jnp.einsum("qhgd,khd->hgqk", query_rot, key_block, preferred_element_type=f32)
        allowed = place_mine[:, None] >= key_place[None, :]
        weights = jnp.where(allowed, jnp.exp(score_scale * raw_scores - log_total[..., None]), 0.0)
        grad_value = jnp.einsum(
            "hgqk,hgqd->khd", weights.astype(bf16), grad_heads, preferred_element_type=f32
        )
        grad_weights = jnp.einsum(
            "hgqd,khd->hgqk", grad_heads, value_block, preferred_element_type=f32
        )
        grad_scores = (weights * (grad_weights - delta[..., None]) * score_scale).astype(bf16)
        grad_query = grad_query + jnp.einsum(
            "hgqk,khd->hgqd", grad_scores, key_block, preferred_element_type=f32
        )
        grad_key = jnp.einsum("hgqk,qhgd->khd", grad_scores, query_rot, preferred_element_type=f32)
        joined = jnp.concatenate(
            [grad_key.reshape(block_rows, kv_width), grad_value.reshape(block_rows, kv_width)],
            axis=1,
        )
        return (grad_query, joined)

    grad_query_acc, joined_blocks = lax.scan(attend_back, grad_query_acc, blocks)
    grad_kv_acc = joined_blocks.reshape(piece_rows, 2 * kv_width)
    grad_query_acc, grad_kv_all = (grad_query_acc, grad_kv_acc)
    grad_kv = summed_on_arrival(grad_kv_all.astype(jnp.bfloat16), "ctx", 0)
    grad_query_rot = jnp.transpose(grad_query_acc, (2, 0, 1, 3)).reshape(tok_rows, HEADS, HEAD_DIM)
    grad_query = rotate(grad_query_rot, -angles).reshape(tok_rows, q_width).astype(bf16)
    grad_key = rotate(grad_kv[:, :kv_width].reshape(tok_rows, KV_HEADS, HEAD_DIM), -angles)
    grad_key = grad_key.reshape(tok_rows, kv_width).astype(bf16)
    grad_value = grad_kv[:, kv_width:].astype(bf16)
    grad_wquery = jnp.einsum("tc,tq->cq", normed, grad_query, preferred_element_type=f32)
    grad_wkey = jnp.einsum("tc,tq->cq", normed, grad_key, preferred_element_type=f32)
    grad_wvalue = jnp.einsum("tc,tq->cq", normed, grad_value, preferred_element_type=f32)
    grad_bquery = jnp.sum(grad_query.astype(f32), axis=0)
    grad_bkey = jnp.sum(grad_key.astype(f32), axis=0)
    grad_bvalue = jnp.sum(grad_value.astype(f32), axis=0)
    grad_normed = (
        jnp.einsum("tq,cq->tc", grad_query, weight_query, preferred_element_type=f32)
        + jnp.einsum("tq,cq->tc", grad_key, weight_key, preferred_element_type=f32)
        + jnp.einsum("tq,cq->tc", grad_value, weight_value, preferred_element_type=f32)
    )
    grad_input_part, grad_gain_one = jax.vjp(rms_scale, inputs, gain_one.astype(f32))[1](
        grad_normed
    )
    input_grad = grad_middle + grad_input_part
    (
        half_gain_one,
        half_wquery,
        half_bquery,
        half_wkey,
        half_bkey,
        half_wvalue,
        half_bvalue,
        half_wout,
        half_gain_two,
        half_gate,
        half_up,
        half_down,
    ) = (
        lax.psum_scatter(
            grad_gain_one.astype(jnp.bfloat16), "fsdp", scatter_dimension=0, tiled=True
        ).astype(jnp.float32),
        lax.psum_scatter(
            grad_wquery.astype(jnp.bfloat16), "fsdp", scatter_dimension=0, tiled=True
        ).astype(jnp.float32),
        lax.psum_scatter(
            grad_bquery.astype(jnp.bfloat16), "fsdp", scatter_dimension=0, tiled=True
        ).astype(jnp.float32),
        lax.psum_scatter(
            grad_wkey.astype(jnp.bfloat16), "fsdp", scatter_dimension=0, tiled=True
        ).astype(jnp.float32),
        lax.psum_scatter(
            grad_bkey.astype(jnp.bfloat16), "fsdp", scatter_dimension=0, tiled=True
        ).astype(jnp.float32),
        lax.psum_scatter(
            grad_wvalue.astype(jnp.bfloat16), "fsdp", scatter_dimension=0, tiled=True
        ).astype(jnp.float32),
        lax.psum_scatter(
            grad_bvalue.astype(jnp.bfloat16), "fsdp", scatter_dimension=0, tiled=True
        ).astype(jnp.float32),
        lax.psum_scatter(
            grad_wout.astype(jnp.bfloat16), "fsdp", scatter_dimension=0, tiled=True
        ).astype(jnp.float32),
        lax.psum_scatter(
            grad_gain_two.astype(jnp.bfloat16), "fsdp", scatter_dimension=0, tiled=True
        ).astype(jnp.float32),
        lax.psum_scatter(
            grad_wgate.astype(jnp.bfloat16), "fsdp", scatter_dimension=0, tiled=True
        ).astype(jnp.float32),
        lax.psum_scatter(
            grad_wup.astype(jnp.bfloat16), "fsdp", scatter_dimension=0, tiled=True
        ).astype(jnp.float32),
        lax.psum_scatter(
            grad_down.astype(jnp.bfloat16), "fsdp", scatter_dimension=0, tiled=True
        ).astype(jnp.float32),
    )
    (
        total_gain_one,
        total_wquery,
        total_bquery,
        total_wkey,
        total_bkey,
        total_wvalue,
        total_bvalue,
        total_wout,
        total_gain_two,
        total_gate,
        total_up,
        total_down,
    ) = lax.psum(
        (
            half_gain_one,
            half_wquery,
            half_bquery,
            half_wkey,
            half_bkey,
            half_wvalue,
            half_bvalue,
            half_wout,
            half_gain_two,
            half_gate,
            half_up,
            half_down,
        ),
        "ctx",
    )
    return (
        layer_output[None],
        input_grad[None],
        total_gain_one,
        total_wquery,
        total_bquery,
        total_wkey,
        total_bkey,
        total_wvalue,
        total_bvalue,
        total_wout,
        total_gain_two,
        total_gate,
        total_up,
        total_down,
    )


def solution(mesh):
    placed = (
        P("fsdp", "ctx", None),
        P("fsdp", "ctx", None),
        P(),
        P("fsdp"),
        P("fsdp", None),
        P("fsdp"),
        P("fsdp", None),
        P("fsdp"),
        P("fsdp", None),
        P("fsdp"),
        P("fsdp", None),
        P("fsdp"),
        P("fsdp", None),
        P("fsdp", None),
        P("fsdp", None),
    )
    return jax.shard_map(
        body,
        mesh=mesh,
        in_specs=placed,
        out_specs=(
            P("fsdp", "ctx", None),
            P("fsdp", "ctx", None),
            P("fsdp"),
            P("fsdp", None),
            P("fsdp"),
            P("fsdp", None),
            P("fsdp"),
            P("fsdp", None),
            P("fsdp"),
            P("fsdp", None),
            P("fsdp"),
            P("fsdp", None),
            P("fsdp", None),
            P("fsdp", None),
        ),
        check_vma=False,
    )
```

profile of v0, /device:TPU:0, one launch (start us, length us, event | category | flops | bytes accessed | tf_op | source)
XLA Modules:
  0.0 1671.8 jit_solution(5590220814165377826)
XLA Ops:
  8.9 2.3 all_gather.41
  18.1 2.5 all-reduce.12
  20.6 2.2 all_gather.43
  31.2 2.2 convolution_add_fusion.4
  33.9 62.5 %all-gather.7.cloned.1.call-done = bf16[4096,256]{0,1:T(8,128)(2,1)} async-done(((bf16[256,256]{0,1:T(8,128)(2,1)}), bf16[4096,256]{0,1:T(8,128)(2,1)}) %all-gather.7.cloned.1.call-update) | async-done | bytes 2097168 | tf_op jit(solution)/shard_map/all_gather | solution.py:148
  101.5 57.7 %while.28 = (s32[]{:T(128)}, f32[2,7,256]{2,1,0:T(8,128)S(1)}, f32[2,7,256]{2,1,0:T(8,128)S(1)}, f32[2,7,256,64]{2,3,1,0:T(8,128)S(1)}, s32[256]{0:T(256)S(1)}, ...) while((s32[]{:T(128)}, f32[2,7,256]{2,1,0:T(8,128)S(1)}, ...), condition=%wide.region_5.6_spmd.clone, body=%wide.region_2.5_spmd.clone.sunk | while | flops 494454272 | bytes 25336972 | solution.py:166
  102.2 2.1 fusion.164
  106.1 3.0 fusion.167
  109.3 2.1 fusion.164
  113.2 3.0 fusion.167
  116.5 2.2 fusion.164
  120.4 3.1 fusion.167
  123.6 2.2 fusion.164
  127.6 3.0 fusion.167
  130.8 2.1 fusion.164
  134.7 3.0 fusion.167
  138.0 2.2 fusion.164
  141.9 3.1 fusion.167
  145.2 2.1 fusion.164
  149.1 3.0 fusion.167
  152.3 2.1 fusion.164
  156.2 3.0 fusion.167
  160.2 2.2 multiply_reduce_fusion.3
  162.6 9.8 fusion.100
  172.5 7.9 fusion.99
  180.3 10.1 multiply_convert_fusion
  190.5 2.8 fusion.101
  193.3 7.1 multiply_reduce_fusion
  203.6 2.2 convolution_convert_fusion.5
  208.3 97.9 %while.29 = (s32[]{:T(128)}, f32[2,7,256,64]{2,3,1,0:T(8,128)S(1)}, bf16[8,512,256]{2,1,0:T(8,128)(2,1)}, s32[256]{0:T(256)S(1)}, s32[8,512]{1,0:T(8,128)S(1)}, ...) while((s32[]{:T(128)}, f32[2,7,256,64]{2,3,1,0:T(8,128)S(1)}, ...), condition=%wide.region_10.11_spmd.clone, body=%wide.region_9.10_spmd.clone.sunk | while | flops 1195704320 | bytes 39371936 | solution.py:234
  208.5 2.1 fusion.178
  210.6 2.6 fusion.180
  213.1 3.6 fusion.179
  220.7 2.1 fusion.178
  222.8 2.6 fusion.180
  225.4 3.6 fusion.179
  233.0 2.1 fusion.178
  235.0 2.6 fusion.180
  237.6 3.6 fusion.179
  245.2 2.1 fusion.178
  247.3 2.6 fusion.180
  249.8 3.6 fusion.179
  257.4 2.1 fusion.178
  259.5 2.6 fusion.180
  262.1 3.6 fusion.179
  269.7 2.1 fusion.178
  271.7 2.6 fusion.180
  274.3 3.6 fusion.179
  284.0 2.6 fusion.180
  286.5 3.6 fusion.179
  294.2 2.1 fusion.178
  296.2 2.6 fusion.180
  298.8 3.6 fusion.179
  306.2 4.8 all-to-all-start
  313.5 40.3 %all-to-all-done = bf16[16,256,256]{2,1,0:T(8,128)(2,1)} async-done(((bf16[16,256,256]{2,1,0:T(8,128)(2,1)}), bf16[16,256,256]{2,1,0:T(8,128)(2,1)}, u32[]{:S(2)}, u32[]{:S(2)}) %all-to-all-start) | async-done | bytes 2097184 | tf_op jit(solution)/shard_map/all_to_all | solution.py:26
  358.8 8.0 convolution_convert_fusion
  366.9 7.7 convolution_convert_fusion.1
  374.9 7.7 convolution_convert_fusion.2
  384.1 3.1 fusion.102
  387.2 8.6 fusion.45
  398.1 2.5 all-reduce.11
  402.2 20.0 %reduce-scatter.18.cloned.1.call-done = bf16[448,4864]{1,0:T(8,128)(2,1)} async-done(((bf16[896,4864]{1,0:T(8,128)(2,1)}), bf16[448,4864]{1,0:T(8,128)(2,1)}) %reduce-scatter.18.cloned.1.call-update) | async-done | bytes 4358160 | tf_op jit(solution)/shard_map/reduce_scatter | solution.py:302
  422.2 21.2 %reduce-scatter.16.cloned.1.call-done = bf16[448,4864]{1,0:T(8,128)(2,1)} async-done(((bf16[896,4864]{1,0:T(8,128)(2,1)}), bf16[448,4864]{1,0:T(8,128)(2,1)}) %reduce-scatter.16.cloned.1.call-update) | async-done | bytes 4358160 | tf_op jit(solution)/shard_map/reduce_scatter | solution.py:299
  443.4 1221.6 %all-reduce.14 = (f32[448]{0:T(512)}, f32[448,896]{1,0:T(8,128)}, f32[448]{0:T(512)}, f32[448,128]{1,0:T(8,128)}, f32[64]{0:T(128)}, /*index=5*/f32[448,128]{1,0...) all-reduce(f32[448]{0:T(512)S(1)} %dynamic-slice_convert_fusion.2, ...), channel_id=1, replica_groups=mesh['ctx'=16,'fsdp'=2] {'ctx'}, use_global_device_ids=true, to_apply=%region_15.16 | all-reduce | flops 7456192 | bytes 44740096 | tf_op jit(solution)/shard_map/psum | solution.py:322
  (259 shorter events, 88.5 us)
Async XLA Ops:
  7.2 24.0 %all-gather.9.cloned.1.call-start = ((), (), s32[]{:S(2)}) async-start(), calls=%async_computation.9 | async-start | bytes 2408448 | tf_op jit(solution)/shard_map/all_gather | solution.py:109
  7.9 88.5 %all-gather.7.cloned.1.call-start = ((), (), s32[]{:S(2)}) async-start(), calls=%async_computation.8 | async-start | bytes 2228224 | tf_op jit(solution)/shard_map/all_gather | solution.py:148
  11.2 19.3 %copy-start.11 = (bf16[896,128]{1,0:T(8,128)(2,1)}, bf16[896,128]{1,0:T(8,128)(2,1)S(1)}, u32[]{:S(2)}) copy-start(bf16[896,128]{1,0:T(8,128)(2,1)S(1)} %all_gather.41) | copy-start | bytes 688132
  22.8 3.7 copy-start.13
  24.0 2.4 copy-start.17
  28.5 130.8 %all-gather.11.cloned.1.call-start = ((), (), s32[]{:S(2)}) async-start(), calls=%async_computation.10 | async-start | bytes 2408448 | tf_op jit(solution)/shard_map/all_gather | solution.py:115
  29.3 133.3 %all-gather.15.cloned.1.call-start = ((), (), s32[]{:S(2)}) async-start(), calls=%async_computation.12 | async-start | bytes 13074432 | tf_op jit(solution)/shard_map/all_gather | solution.py:175
  29.9 1.4 copy-start
  29.9 142.6 %all-gather.13.cloned.1.call-start = ((), (), s32[]{:S(2)}) async-start(), calls=%async_computation.11 | async-start | bytes 13074432 | tf_op jit(solution)/shard_map/all_gather | solution.py:174
  30.5 149.9 %all-gather.17.cloned.1.call-start = ((), (), s32[]{:S(2)}) async-start(), calls=%async_computation.13 | async-start | bytes 13074432 | tf_op jit(solution)/shard_map/all_gather | solution.py:176
  31.0 364.8 %reduce-scatter.14.cloned.1.call-start = ((), (), s32[]{:S(2)}) async-start(), calls=%async_computation.17 | async-start | bytes 2408448 | tf_op jit(solution)/shard_map/reduce_scatter | solution.py:293
  98.1 3.4 copy-start.5
  159.2 0.9 copy-start.6
  162.4 30.9 %copy-start.3 = (f32[256,896]{1,0:T(8,128)}, f32[256,896]{1,0:T(8,128)S(1)}, u32[]{:S(2)}) copy-start(f32[256,896]{1,0:T(8,128)S(1)} %get-tuple-element.368) | copy-start | bytes 2752516
  180.3 10.2 copy-start.2
  190.5 2.8 copy-start.7
  190.5 2.8 copy-start.8
  193.3 7.1 copy-start.9
  208.3 102.8 %copy-start.15 = (f32[256,32]{0,1:T(8,128)S(1)}, f32[256,32]{0,1:T(8,128)}, u32[]{:S(2)}) copy-start(f32[256,32]{0,1:T(8,128)} %get-tuple-element.361) | copy-start | bytes 98308
  208.3 102.8 %copy-start.16 = (f32[256,32]{0,1:T(8,128)S(1)}, f32[256,32]{0,1:T(8,128)}, u32[]{:S(2)}) copy-start(f32[256,32]{0,1:T(8,128)} %get-tuple-element.363) | copy-start | bytes 98308
  306.2 5.2 copy-start.1
  306.2 47.5 %all-to-all-start = ((bf16[16,256,256]{2,1,0:T(8,128)(2,1)}), bf16[16,256,256]{2,1,0:T(8,128)(2,1)}, u32[]{:S(2)}, u32[]{:S(2)}) async-start(bf16[16,256,256]{2,1,0:T(8,128)(2,1)} %bitcast.250), calls=%async_computation | async-start | bytes 4194304 | tf_op jit(solution)/shard_map/all_to_all | solution.py:26
  311.0 84.8 %reduce-scatter.8.cloned.1.call-start = ((), (), s32[]{:S(2)}) async-start(), calls=%async_computation.14 | async-start | bytes 2408448 | tf_op jit(solution)/shard_map/reduce_scatter | solution.py:275
  311.4 47.4 %copy-start.10 = (bf16[1,256,896]{2,1,0:T(8,128)(2,1)S(1)}, bf16[1,256,896]{2,1,0:T(8,128)(2,1)}, u32[]{:S(2)}) copy-start(bf16[1,256,896]{2,1,0:T(8,128)(2,1)} %param.20) | copy-start | bytes 1376260
  313.4 88.7 %reduce-scatter.12.cloned.1.call-start = ((), (), s32[]{:S(2)}) async-start(), calls=%async_computation.16 | async-start | bytes 344064 | tf_op jit(solution)/shard_map/reduce_scatter | solution.py:287
  356.9 45.2 %reduce-scatter.10.cloned.1.call-start = ((), (), s32[]{:S(2)}) async-start(), calls=%async_computation.15 | async-start | bytes 344064 | tf_op jit(solution)/shard_map/reduce_scatter | solution.py:281
  358.7 43.4 %reduce-scatter.20.cloned.1.call-start = ((), (), s32[]{:S(2)}) async-start(), calls=%async_computation.20 | async-start | bytes 13074432 | tf_op jit(solution)/shard_map/reduce_scatter | solution.py:305
  366.8 55.3 %reduce-scatter.18.cloned.1.call-start = ((), (), s32[]{:S(2)}) async-start(), calls=%async_computation.19 | async-start | bytes 13074432 | tf_op jit(solution)/shard_map/reduce_scatter | solution.py:302
  374.6 68.8 %reduce-scatter.16.cloned.1.call-start = ((), (), s32[]{:S(2)}) async-start(), calls=%async_computation.18 | async-start | bytes 13074432 | tf_op jit(solution)/shard_map/reduce_scatter | solution.py:299
  382.6 4.6 copy-start.4
  387.2 8.6 copy-start.20
  387.2 8.7 copy-start.12
  387.2 10.4 copy-start.14
  387.2 10.9 copy-start.19
  387.2 13.7 copy-start.18
Sparse Core Ops, SparseCore 0:
  9.6 12.5 all-gather.8
  28.7 67.7 all-gather.6
  98.0 8.2 all-gather.10
  107.7 22.1 all-gather.14
  131.3 22.1 all-gather.12
  154.9 22.1 all-gather.16
  208.4 7.4 reduce-scatter.13
  314.7 10.2 reduce-scatter.7
  357.0 11.8 reduce-scatter.11
  371.0 8.7 reduce-scatter.9
  382.7 18.2 reduce-scatter.19
  403.8 18.2 reduce-scatter.17
  425.0 18.2 reduce-scatter.15
where the time goes:
time: 1680 us; the launch traced here: 1670 us
  blocking collectives  1230 us (73%)
  matrix products  221 us (13%)
  waiting for transfers between devices  147 us (9%)
  other arithmetic  28 us (2%)
  local copies, waits for them, and re-layouts  20.1 us (1%)
  between operations  17.4 us (1%)
    psum x1, blocking collectives, body(): lax.psum((half_gain_one, half_wquery, half_bquery, half_wkey, half_bkey,...  1220 us
    all_gather x1, waiting for transfers between devices, body(): lax.all_gather(kv_local, 'ctx', axis=0, tiled=True)  62.5 us
    all_to_all x1, waiting for transfers between devices, summed_on_arrival(): lax.all_to_all(cut_along(array, dim, peers), axis, 0, 0, tiled=True)  40.3 us
  transfers between devices with their start and end apart: 14, of which 4 were waited for; matrix products, arithmetic and copies ran while one was open for 14% of the time, Pallas kernels for 0%

commit v1 on v0

--- a/solution.py
+++ b/solution.py
@@ -1,8 +1,12 @@
+import functools
 import math
 
 import jax
 import jax.numpy as jnp
+import numpy as np
 from jax import lax
+from jax.experimental import pallas as pl
+from jax.experimental.pallas import tpu as pltpu
 from jax.sharding import PartitionSpec as P
 
 HEADS = 14
@@ -15,16 +19,226 @@
 NEGATIVE = -1e30
 
 
-def cut_along(array, dim, peers):
-    shape = array.shape
-    blocks = array.reshape(*shape[:dim], peers, shape[dim] // peers, *shape[dim + 1 :])
-    return jnp.moveaxis(blocks, dim, 0)
-
-
-def summed_on_arrival(array, axis, dim):
-    peers = lax.axis_size(axis)
-    blocks = lax.all_to_all(cut_along(array, dim, peers), axis, 0, 0, tiled=True)
-    return jnp.sum(blocks.astype(jnp.float32), axis=0)
+LANE_SHARES = (0.4, 0.4, 0.2)
+
+
+def lane_orders(ctx_count):
+    bits = list(range(ctx_count.bit_length() - 1))
+    return (bits, [1, 0] + bits[2:], bits[2:] + bits[:2])
+
+
+def lane_chunks(units, splits, ctx_count):
+    orders = lane_orders(ctx_count)
+    third = max(1, round(units * LANE_SHARES[2]))
+    first = (units - third + 1) // 2
+    counts = (first, units - third - first, third)
+    lists = []
+    for order, count, parts in zip(orders, counts, splits):
+        parts = min(parts, count)
+        sizes = [count // parts + (1 if i < count % parts else 0) for i in range(parts)]
+        lists.append([(size, order) for size in sizes])
+    chunks = []
+    start = 0
+    for level in range(max(len(items) for items in lists)):
+        for items in lists:
+            if level < len(items):
+                size, order = items[level]
+                chunks.append((start, size, order))
+                start += size
+    return chunks
+
+
+def bit_of(index, bit):
+    return lax.rem(index // (1 << bit), 2)
+
+
+def exchange_kernel(chunks, ctx_count, fsdp_sum, scatter, gather, *refs):
+    stages = ctx_count.bit_length() - 1
+    unit = 16 * ctx_count
+    refs = list(refs)
+    source, result = refs[0], refs[1]
+    scratch = refs[2:]
+    me = lax.axis_index("ctx")
+    core = lax.axis_index("fsdp")
+    partners = [me + (1 << b) * (1 - 2 * bit_of(me, b)) for b in range(stages)]
+    total = sum(size for _, size, _ in chunks) * unit
+    mesh_id = pl.DeviceIdType.MESH
+
+    barrier = pltpu.get_barrier_semaphore()
+    for partner in partners:
+        pl.semaphore_signal(
+            barrier, inc=1, device_id={"ctx": partner}, device_id_type=mesh_id
+        )
+    if fsdp_sum:
+        pl.semaphore_signal(
+            barrier, inc=1, device_id={"fsdp": 1 - core}, device_id_type=mesh_id
+        )
+    pl.semaphore_wait(barrier, stages + (1 if fsdp_sum else 0))
+
+    def rows(start, size):
+        return pl.ds(pl.multiple_of(start, 16), size)
+
+    def places(chunk):
+        start, size, order = chunk
+        low = start * unit
+        span = size * unit
+        found = []
+        for bit in order:
+            half = span // 2
+            mine = bit_of(me, bit)
+            found.append((low + mine * half, low + (1 - mine) * half, half, bit))
+            low = low + mine * half
+            span = half
+        return found, low, span
+
+    plans = [places(chunk) for chunk in chunks]
+    pending = []
+
+    def remote(src, dst, sems, c, s, target):
+        copy = pltpu.make_async_remote_copy(
+            src_ref=src,
+            dst_ref=dst,
+            send_sem=sems[0].at[c, s],
+            recv_sem=sems[1].at[c, s],
+            device_id=target,
+            device_id_type=mesh_id,
+        )
+        copy.start()
+        pending.append(copy)
+        return copy
+
+    def add_rows(own, low, other, low_other, size):
+        block = 16 * max(d for d in (1, 2, 3, 4) if (size // 16) % d == 0)
+
+        @pl.loop(0, size // block)
+        def _(i):
+            here = rows(low + i * block, block)
+            own[here, :] = own[here, :] + other[rows(low_other + i * block, block), :]
+
+    if scatter:
+        own, landings, local_sems = scratch[0], scratch[1 : 1 + stages], scratch[1 + stages]
+        rs_sems = scratch[2 + stages : 4 + stages]
+        rest = scratch[4 + stages :]
+        if fsdp_sum:
+            first_landing, rest = rest[0], rest[1:]
+            fs_sems, rest = rest[:2], rest[2:]
+        loads, firsts = [], []
+        for c, (start, size, _) in enumerate(chunks):
+            low, span = start * unit, size * unit
+            if fsdp_sum:
+                firsts.append(
+                    remote(
+                        source.at[rows((1 - core) * total + low, span)],
+                        first_landing.at[rows(low, span)],
+                        fs_sems,
+                        c,
+                        0,
+                        {"fsdp": 1 - core},
+                    )
+                )
+            base = core * total if fsdp_sum else 0
+            load = pltpu.make_async_copy(
+                source.at[rows(base + low, span)], own.at[rows(low, span)], local_sems.at[c]
+            )
+            load.start()
+            loads.append(load)
+        arrivals = {}
+        for s in range(stages + 1):
+            for c, (start, size, _) in enumerate(chunks):
+                found, low_end, span_end = plans[c]
+                if s == 0:
+                    loads[c].wait()
+                    if fsdp_sum:
+                        firsts[c].wait_recv()
+                        add_rows(own, start * unit, first_landing, start * unit, size * unit)
+                else:
+                    keep, _, half, _ = found[s - 1]
+                    arrivals[c].wait_recv()
+                    add_rows(own, keep, landings[s - 1], (start * unit) >> s, half)
+                if s < stages:
+                    _, send, half, bit = found[s]
+                    arrivals[c] = remote(
+                        own.at[rows(send, half)],
+                        landings[s].at[rows((start * unit) >> (s + 1), half)],
+                        rs_sems,
+                        c,
+                        s,
+                        {"ctx": partners[bit]},
+                    )
+                else:
+                    target = low_end if gather else start * 16
+                    store = pltpu.make_async_copy(
+                        own.at[rows(low_end, span_end)],
+                        result.at[rows(target, span_end)],
+                        local_sems.at[c],
+                    )
+                    store.start()
+                    loads[c] = store
+    else:
+        local_sems, rest = scratch[0], scratch[1:]
+        loads = []
+        for c, (start, size, _) in enumerate(chunks):
+            _, low_end, span_end = plans[c]
+            store = pltpu.make_async_copy(
+                source.at[rows(start * 16, size * 16)],
+                result.at[rows(low_end, span_end)],
+                local_sems.at[c],
+            )
+            store.start()
+            loads.append(store)
+    if gather:
+        ag_sems = rest[:2]
+        arrivals = {}
+        for s in range(stages + 1):
+            for c in range(len(chunks)):
+                found, _, _ = plans[c]
+                if s == 0:
+                    loads[c].wait()
+                else:
+                    arrivals[c].wait_recv()
+                if s < stages:
+                    keep, _, half, bit = found[stages - 1 - s]
+                    region = result.at[rows(keep, half)]
+                    arrivals[c] = remote(
+                        region, region, ag_sems, c, s, {"ctx": partners[bit]}
+                    )
+    else:
+        for load in loads:
+            load.wait()
+    for copy in pending:
+        copy.wait_send()
+
+
+def exchange(source, chunks, ctx_count, collective_id, fsdp_sum, scatter, gather):
+    stages = ctx_count.bit_length() - 1
+    unit = 16 * ctx_count
+    columns = source.shape[1]
+    total = sum(size for _, size, _ in chunks) * unit
+    bf16 = jnp.bfloat16
+    count = len(chunks)
+    dma = pltpu.SemaphoreType.DMA
+    scratch = []
+    if scatter:
+        scratch.append(pltpu.VMEM((total, columns), bf16))
+        scratch += [pltpu.VMEM((total >> (s + 1), columns), bf16) for s in range(stages)]
+        scratch += [dma((count,)), dma((count, stages)), dma((count, stages))]
+        if fsdp_sum:
+            scratch += [pltpu.VMEM((total, columns), bf16), dma((count, 1)), dma((count, 1))]
+    else:
+        scratch.append(dma((count,)))
+    if gather:
+        scratch += [dma((count, stages)), dma((count, stages))]
+    out_rows = total if gather else total // ctx_count
+    return pl.pallas_call(
+        functools.partial(exchange_kernel, chunks, ctx_count, fsdp_sum, scatter, gather),
+        out_shape=jax.ShapeDtypeStruct((out_rows, columns), bf16),
+        in_specs=[pl.BlockSpec(memory_space=pl.ANY)],
+        out_specs=pl.BlockSpec(memory_space=pl.ANY),
+        scratch_shapes=scratch,
+        compiler_params=pltpu.CompilerParams(
+            collective_id=collective_id, has_side_effects=True, vmem_limit_bytes=56 * 2**20
+        ),
+    )(source)
 
 
 def rms_scale(values, gain_vec):
@@ -55,15 +269,24 @@
     )
 
 
-def place_table(span_perm, tok_rows, ctx_count):
-    row_ids = jnp.arange(tok_rows * ctx_count, dtype=jnp.int32)
-    owner_dev = row_ids // tok_rows
-    within = row_ids % tok_rows
+def place_table(span_perm, owner_dev, within, tok_rows, ctx_count):
     matches = owner_dev[:, None] == jnp.arange(ctx_count, dtype=jnp.int32)[None, :]
     first_span = jnp.sum(jnp.where(matches, span_perm[None, :], 0), axis=1)
     half_rows = tok_rows // 2
     span_id = jnp.where(within < half_rows, first_span, 2 * ctx_count - 1 - first_span)
     return span_id * half_rows + within % half_rows
+
+
+def gathered_order(chunks, ctx_count):
+    owners, tokens = [], []
+    for start, size, order in chunks:
+        slots = np.arange(ctx_count)
+        device = np.zeros(ctx_count, np.int64)
+        for k, bit in enumerate(order):
+            device |= ((slots >> (len(order) - 1 - k)) & 1) << bit
+        owners.append(np.repeat(device, size * 16))
+        tokens.append(np.tile(np.arange(start * 16, (start + size) * 16), ctx_count))
+    return np.concatenate(owners).astype(np.int32), np.concatenate(tokens).astype(np.int32)
 
 
 def body(
@@ -92,8 +315,15 @@
     kv_width = KV_HEADS * HEAD_DIM
     q_width = HEADS * HEAD_DIM
     score_scale = 1.0 / math.sqrt(HEAD_DIM)
-    place_all = place_table(span_perm, tok_rows, ctx_count)
-    place_mine = lax.dynamic_slice_in_dim(place_all, ctx_index * tok_rows, tok_rows)
+    kv_chunks = lane_chunks(tok_rows // 16, (1, 1, 1), ctx_count)
+    key_owner, key_token = gathered_order(kv_chunks, ctx_count)
+    place_all = place_table(
+        span_perm, jnp.asarray(key_owner), jnp.asarray(key_token), tok_rows, ctx_count
+    )
+    own_rows = jnp.arange(tok_rows, dtype=jnp.int32)
+    place_mine = place_table(
+        span_perm, jnp.full((tok_rows,), ctx_index), own_rows, tok_rows, ctx_count
+    )
     angles = angle_table(place_mine, HEAD_DIM)
     (
         gain_one,
@@ -144,9 +374,8 @@
         jnp.zeros((KV_HEADS, group_size, tok_rows, HEAD_DIM), f32),
     )
     carried = start_state
-    piece_rows, block_rows, blocks = split_piece(
-        lax.all_gather(kv_local, "ctx", axis=0, tiled=True)
-    )
+    kv_all = exchange(kv_local, kv_chunks, ctx_count, 1, False, False, True)
+    piece_rows, block_rows, blocks = split_piece(kv_all)
 
     def attend_block(inner, block_data):
         run_max, run_sum, run_out = inner
@@ -205,9 +434,6 @@
     )
     delta = jnp.sum(grad_heads.astype(f32) * attn_heads, axis=-1)
     grad_query_acc = jnp.zeros((KV_HEADS, group_size, tok_rows, HEAD_DIM), f32)
-    piece_rows, block_rows, blocks = split_piece(
-        lax.all_gather(kv_local, "ctx", axis=0, tiled=True)
-    )
 
     def attend_back(grad_query, block_data):
         key_block, value_block, key_place = block_data
@@ -234,7 +460,9 @@
     grad_query_acc, joined_blocks = lax.scan(attend_back, grad_query_acc, blocks)
     grad_kv_acc = joined_blocks.reshape(piece_rows, 2 * kv_width)
     grad_query_acc, grad_kv_all = (grad_query_acc, grad_kv_acc)
-    grad_kv = summed_on_arrival(grad_kv_all.astype(jnp.bfloat16), "ctx", 0)
+    grad_kv = exchange(
+        grad_kv_all.astype(bf16), kv_chunks, ctx_count, 2, False, True, False
+    ).astype(f32)
     grad_query_rot = jnp.transpose(grad_query_acc, (2, 0, 1, 3)).reshape(tok_rows, HEADS, HEAD_DIM)
     grad_query = rotate(grad_query_rot, -angles).reshape(tok_rows, q_width).astype(bf16)
     grad_key = rotate(grad_kv[:, :kv_width].reshape(tok_rows, KV_HEADS, HEAD_DIM), -angles)
@@ -255,87 +483,74 @@
         grad_normed
     )
     input_grad = grad_middle + grad_input_part
-    (
-        half_gain_one,
-        half_wquery,
-        half_bquery,
-        half_wkey,
-        half_bkey,
-        half_wvalue,
-        half_bvalue,
-        half_wout,
-        half_gain_two,
-        half_gate,
-        half_up,
-        half_down,
-    ) = (
-        lax.psum_scatter(
-            grad_gain_one.astype(jnp.bfloat16), "fsdp", scatter_dimension=0, tiled=True
-        ).astype(jnp.float32),
-        lax.psum_scatter(
-            grad_wquery.astype(jnp.bfloat16), "fsdp", scatter_dimension=0, tiled=True
-        ).astype(jnp.float32),
-        lax.psum_scatter(
-            grad_bquery.astype(jnp.bfloat16), "fsdp", scatter_dimension=0, tiled=True
-        ).astype(jnp.float32),
-        lax.psum_scatter(
-            grad_wkey.astype(jnp.bfloat16), "fsdp", scatter_dimension=0, tiled=True
-        ).astype(jnp.float32),
-        lax.psum_scatter(
-            grad_bkey.astype(jnp.bfloat16), "fsdp", scatter_dimension=0, tiled=True
-        ).astype(jnp.float32),
-        lax.psum_scatter(
-            grad_wvalue.astype(jnp.bfloat16), "fsdp", scatter_dimension=0, tiled=True
-        ).astype(jnp.float32),
-        lax.psum_scatter(
-            grad_bvalue.astype(jnp.bfloat16), "fsdp", scatter_dimension=0, tiled=True
-        ).astype(jnp.float32),
-        lax.psum_scatter(
-            grad_wout.astype(jnp.bfloat16), "fsdp", scatter_dimension=0, tiled=True
-        ).astype(jnp.float32),
-        lax.psum_scatter(
-            grad_gain_two.astype(jnp.bfloat16), "fsdp", scatter_dimension=0, tiled=True
-        ).astype(jnp.float32),
-        lax.psum_scatter(
-            grad_wgate.astype(jnp.bfloat16), "fsdp", scatter_dimension=0, tiled=True
-        ).astype(jnp.float32),
-        lax.psum_scatter(
-            grad_wup.astype(jnp.bfloat16), "fsdp", scatter_dimension=0, tiled=True
-        ).astype(jnp.float32),
-        lax.psum_scatter(
-            grad_down.astype(jnp.bfloat16), "fsdp", scatter_dimension=0, tiled=True
-        ).astype(jnp.float32),
-    )
-    (
-        total_gain_one,
-        total_wquery,
-        total_bquery,
-        total_wkey,
-        total_bkey,
-        total_wvalue,
-        total_bvalue,
-        total_wout,
-        total_gain_two,
-        total_gate,
-        total_up,
-        total_down,
-    ) = lax.psum(
-        (
-            half_gain_one,
-            half_wquery,
-            half_bquery,
-            half_wkey,
-            half_bkey,
-            half_wvalue,
-            half_bvalue,
-            half_wout,
-            half_gain_two,
-            half_gate,
-            half_up,
-            half_down,
-        ),
-        "ctx",
-    )
+    width = layer_input.shape[2]
+    half = width // 2
+
+    def halves(array):
+        return array.astype(bf16).reshape(2, array.shape[0] // 2, *array.shape[1:])
+
+    gate_parts, up_parts = halves(grad_wgate), halves(grad_wup)
+    whole_blocks = gate_parts.shape[2] // width
+    body_cols = whole_blocks * width
+    tail_cols = gate_parts.shape[2] - body_cols
+    kv_rows = half * kv_width // width
+    vectors = jnp.concatenate(
+        [
+            halves(item)
+            for item in (grad_gain_one, grad_bquery, grad_gain_two, grad_bkey, grad_bvalue)
+        ],
+        axis=1,
+    )
+    vectors = jnp.pad(vectors, ((0, 0), (0, 16 * width - vectors.shape[1]))).reshape(2, 16, width)
+    value_rows = halves(grad_wvalue).reshape(2, width // kv_width, kv_rows, kv_width)
+    pieces = [halves(grad_down)]
+    for parts in (gate_parts, up_parts):
+        pieces += [parts[:, :, i * width : (i + 1) * width] for i in range(whole_blocks)]
+    pieces.append(
+        jnp.concatenate(
+            [gate_parts[:, :, body_cols:], up_parts[:, :, body_cols:], halves(grad_wkey)], axis=2
+        )
+    )
+    pieces += [halves(grad_wquery), halves(grad_wout)]
+    pieces.append(jnp.concatenate([value_rows[:, i] for i in range(width // kv_width)], axis=2))
+    pieces.append(vectors)
+    used = sum(piece.shape[1] for piece in pieces)
+    unit = 16 * ctx_count
+    padded = -(-used // unit) * unit
+    if padded > used:
+        pieces.append(jnp.zeros((2, padded - used, width), bf16))
+    packed = jnp.concatenate(pieces, axis=1).reshape(2 * padded, width)
+    chunks = lane_chunks(padded // unit, (4, 4, 2), ctx_count)
+    summed = exchange(packed, chunks, ctx_count, 3, True, True, True)
+    ff_half = grad_down.shape[0] // 2
+    total_down = summed[:ff_half].astype(f32)
+    at = ff_half
+    blocks_of = []
+    for i in range(2 * whole_blocks + 3):
+        blocks_of.append(summed[at : at + half])
+        at += half
+    tail = blocks_of[2 * whole_blocks]
+    total_gate = jnp.concatenate(
+        blocks_of[:whole_blocks] + [tail[:, :tail_cols]], axis=1
+    ).astype(f32)
+    total_up = jnp.concatenate(
+        blocks_of[whole_blocks : 2 * whole_blocks] + [tail[:, tail_cols : 2 * tail_cols]], axis=1
+    ).astype(f32)
+    total_wkey = tail[:, 2 * tail_cols :].astype(f32)
+    total_wquery = blocks_of[2 * whole_blocks + 1].astype(f32)
+    total_wout = blocks_of[2 * whole_blocks + 2].astype(f32)
+    value_sum = summed[at : at + kv_rows]
+    total_wvalue = jnp.concatenate(
+        [value_sum[:, i * kv_width : (i + 1) * kv_width] for i in range(width // kv_width)], axis=0
+    ).astype(f32)
+    at += kv_rows
+    flat = summed[at : at + 16].reshape(16 * width).astype(f32)
+    kv_half = kv_width // 2
+    total_gain_one = flat[:half]
+    total_bquery = flat[half : 2 * half]
+    total_gain_two = flat[2 * half : 3 * half]
+    total_bkey = flat[3 * half : 3 * half + kv_half]
+    total_bvalue = flat[3 * half + kv_half : 3 * half + 2 * kv_half]
     return (
         layer_output[None],
         input_grad[None],

time: 1680 us -> 820 us (0.49)
  blocking collectives: 1230 us -> 6.91 us
  Pallas kernels: 0 us -> 346 us
  waiting for transfers between devices: 147 us -> 3.14 us
  local copies, waits for them, and re-layouts: 20.1 us -> 87.1 us
  other arithmetic: 28 us -> 83.3 us
  matrix products: 221 us -> 271 us
    psum x1 -> x0, blocking collectives: 1220 us -> none  [body(): lax.psum((half_gain_one, half_wquery, half_bquery, half_wkey, half_bkey,...]
    pallas_call x0 -> x3, Pallas kernels: none -> 346 us  [exchange(): pl.pallas_call(functools.partial(exchange_kernel, chunks, ctx_count, fsdp...]
    all_gather x1 -> x0, waiting for transfers between devices: 62.5 us -> none  [body(): lax.all_gather(kv_local, 'ctx', axis=0, tiled=True)]
    unnamed x57 -> x166, local copies, waits for them, and re-layouts: 9.88 us -> 62.2 us
    reduce_scatter x7 -> x0, waiting for transfers between devices: 41.2 us -> none  [the longest x1 21.2 us: body(): lax.psum_scatter(grad_wgate.astype(jnp.bfloat16), 'fsdp', scatter_dimensi...]
    all_to_all x1 -> x0, waiting for transfers between devices: 40.3 us -> none  [summed_on_arrival(): lax.all_to_all(cut_along(array, dim, peers), axis, 0, 0, tiled=True)]
    reduce_sum x8, other arithmetic: 13.7 us -> 40.8 us  [attend_block(): run_sum = factor * run_sum + jnp.sum(weights, axis=-1)]
    convert_element_type x5 -> x6, other arithmetic: 0.37 us -> 18.9 us  [the longest x1 6.45 us: body(): total_down = summed[:ff_half].astype(f32)]
  transfers between devices with their start and end apart: 14 -> 5, of which waited for: 4 -> 0; matrix products, arithmetic and copies ran while one was open for 14% -> 20% of each run, Pallas kernels for 0% -> 4%
where the time goes in v1:
time: 820 us; the launch traced here: 815 us
  Pallas kernels  346 us (42%)
  matrix products  271 us (33%)
  local copies, waits for them, and re-layouts  87.1 us (11%)
  other arithmetic  83.3 us (10%)
  between operations  16.2 us (2%)
    pallas_call x3, Pallas kernels, exchange(): pl.pallas_call(functools.partial(exchange_kernel, chunks, ctx_count, fsdp...  346 us
    unnamed x166, local copies, waits for them, and re-layouts  62.2 us
    reduce_sum x8, other arithmetic, attend_block(): run_sum = factor * run_sum + jnp.sum(weights, axis=-1)  40.8 us
    dot_general x8, matrix products, attend_back(): jnp.einsum('hgqd,khd->hgqk', grad_heads, value_block, preferred_element_t...  40.2 us
    dot_general x8, matrix products, attend_back(): jnp.einsum('hgqk,hgqd->khd', weights.astype(bf16), grad_heads, preferred_...  36.6 us
    dot_general x8, matrix products, attend_block(): jnp.einsum('qhgd,khd->hgqk', query_rot, key_block, preferred_element_type...  34 us
    dot_general x8, matrix products, attend_block(): jnp.einsum('hgqk,khd->hgqd', weights.astype(bf16), value_block, preferred...  33.1 us
    dot_general x8, matrix products, attend_back(): jnp.einsum('hgqk,khd->hgqd', grad_scores, key_block, preferred_element_ty...  24.5 us
  transfers between devices with their start and end apart: 5, of which 0 were waited for; matrix products, arithmetic and copies ran while one was open for 20% of the time, Pallas kernels for 4%

profile of v1, /device:TPU:0, one launch (start us, length us, event | category | flops | bytes accessed | tf_op | source)
XLA Modules:
  0.0 814.8 jit_solution(9693037991158441688)
XLA Ops:
  23.9 34.4 %shard_map.272 = bf16[4096,256]{1,0:T(8,128)(2,1)} custom-call(bf16[256,256]{1,0:T(8,128)(2,1)} %pad_maximum_fusion.1.refs_0_), custom_call_target="tpu_custom_call" | custom-call | tf_op jit(solution)/shard_map/pallas_call | solution.py:232
  62.7 4.7 copy.87
  67.4 5.1 reshape.391
  72.5 6.0 copy.88
  78.5 3.1 convolution_add_fusion.4
  85.4 112.3 %while.28 = (s32[]{:T(128)}, f32[2,7,256]{2,1,0:T(8,128)S(1)}, f32[2,7,256]{2,1,0:T(8,128)S(1)}, f32[2,7,256,64]{2,3,1,0:T(8,128)}, s32[256]{0:T(256)S(1)}, /*in...) while((s32[]{:T(128)}, f32[2,7,256]{2,1,0:T(8,128)S(1)}, ...), condition=%wide.region_6.7_spmd.clone, body=%wide.region_3.6_spmd.clone.sunk | while | flops 494454272 | bytes 54697128 | solution.py:395
  85.5 4.3 fusion.160
  89.8 6.1 fusion.161
  97.4 3.9 fusion.163
  101.4 4.3 fusion.160
  105.7 4.9 fusion.161
  110.9 4.2 fusion.163
  115.2 4.3 fusion.160
  119.5 4.9 fusion.161
  124.6 4.2 fusion.163
  129.0 4.3 fusion.160
  133.2 4.9 fusion.161
  138.4 4.2 fusion.163
  142.8 4.3 fusion.160
  147.0 4.9 fusion.161
  152.2 4.2 fusion.163
  156.5 4.3 fusion.160
  160.8 4.9 fusion.161
  165.9 4.2 fusion.163
  170.3 4.3 fusion.160
  174.6 4.9 fusion.161
  179.7 4.2 fusion.163
  184.1 4.3 fusion.160
  188.3 4.9 fusion.161
  193.5 4.2 fusion.163
  203.6 7.9 fusion.94
  211.5 8.3 %fusion.95 = f32[256,4864]{1,0:T(8,128)} fusion(bf16[256,896]{1,0:T(8,128)(2,1)S(1)} %multiply_convert_fusion.2, bf16[896,4864]{1,0:T(8,128)(2,1)} %all-gather.12.cloned.1.call-done), kind=kOutput, calls=%fused_computation.213 | convolution fusion | flops 2231369728 | bytes 14155776 | tf_op jit(solution)/shard_map/dot_general | solution.py:409
  219.8 11.2 %multiply_convert_fusion = (bf16[256,4864]{1,0:T(8,128)(2,1)S(1)}, bf16[256,4864]{1,0:T(8,128)(2,1)S(1)}, bf16[256,4864]{1,0:T(8,128)(2,1)}) fusion(f32[256,4864]{1,0:T(8,128)} %fusion.94, f32[256,4864]{1,0:T(8,128)} %fusion.95, bf16[4864,896]{1,0:T(8,128)(2,1)} %all-gather.14.cloned.1.call-done, bf16[1,256,896]{2,1,0:T(8,128)(2,1)S(1)} %copy-done.18), kind=kOutput, calls=%fused_computation.58 | convolution fusion | flops 2251292672 | bytes 26607616 | tf_op jit(solution)/shard_map/td,fd->tf/dot_general | solution.py:414
  231.0 6.4 convolution_convert_fusion.1
  237.4 6.0 convolution_convert_fusion
  243.5 5.5 fusion.96
  249.0 4.3 multiply_reduce_fusion
  257.8 135.2 %while.29 = (s32[]{:T(128)}, f32[2,7,256,64]{2,3,1,0:T(8,128)S(1)}, bf16[8,512,256]{1,2,0:T(8,128)(2,1)}, s32[256]{0:T(256)S(1)}, s32[8,512]{1,0:T(8,128)S(1)}, ...) while((s32[]{:T(128)}, f32[2,7,256,64]{2,3,1,0:T(8,128)S(1)}, ...), condition=%wide.region_11.12_spmd.clone, body=%wide.region_10.11_spmd.clone.sunk | while | flops 1195704320 | bytes 82363616 | solution.py:460
  260.2 5.0 fusion.175
  268.3 4.6 fusion.176
  277.0 5.0 fusion.175
  285.1 4.6 fusion.176
  293.9 5.0 fusion.175
  302.0 4.6 fusion.176
  310.8 5.0 fusion.175
  318.9 4.6 fusion.176
  327.7 5.0 fusion.175
  335.8 4.6 fusion.176
  344.6 5.0 fusion.175
  352.7 4.6 fusion.176
  361.4 5.0 fusion.175
  369.5 4.6 fusion.176
  378.3 5.0 fusion.175
  386.4 4.6 fusion.176
  392.9 3.9 copy.92
  396.9 28.4 %shard_map.273 = bf16[256,256]{1,0:T(8,128)(2,1)} custom-call(bf16[4096,256]{1,0:T(8,128)(2,1)} %bitcast.304), custom_call_target="tpu_custom_call" | custom-call | tf_op jit(solution)/shard_map/pallas_call | solution.py:232
  435.7 5.3 convolution_convert_fusion.2
  441.0 7.6 constant_dynamic-update-slice_fusion.10
  480.6 283.6 %shard_map.274 = bf16[8448,896]{1,0:T(8,128)(2,1)} custom-call(bf16[16896,896]{1,0:T(8,128)(2,1)} %bitcast.282), custom_call_target="tpu_custom_call" | custom-call | tf_op jit(solution)/shard_map/pallas_call | solution.py:232
  771.3 6.4 slice_convert_fusion
  787.8 3.9 slice_dynamic-update-slice_fusion.10
  792.9 4.4 convert_element_type.252
  797.3 5.0 convert_element_type.253
  804.5 3.6 fusion.46
  (397 shorter events, 158.1 us)
Async XLA Ops:
  7.2 71.3 %all-gather.6.cloned.1.call-start = ((), (), s32[]{:S(2)}) async-start(), calls=%async_computation | async-start | bytes 2408448 | tf_op jit(solution)/shard_map/all_gather | solution.py:339
  8.0 7.1 copy-start.45
  8.0 7.3 copy-start.46
  8.0 7.6 copy-start.42
  8.0 7.8 copy-start.43
  8.0 8.0 copy-start.44
  8.0 10.8 %copy-start.5 = (bf16[1,256,896]{2,1,0:T(8,128)(2,1)S(1)}, bf16[1,256,896]{2,1,0:T(8,128)(2,1)}, u32[]{:S(2)}) copy-start(bf16[1,256,896]{2,1,0:T(8,128)(2,1)} %param.21) | copy-start | bytes 1376260
  8.0 11.0 %copy-start.31 = (bf16[448,128]{1,0:T(8,128)(2,1)S(1)}, bf16[448,128]{1,0:T(8,128)(2,1)}, u32[]{:S(2)}) copy-start(bf16[448,128]{1,0:T(8,128)(2,1)} %param.27) | copy-start | bytes 344068
  8.1 192.0 %all-gather.8.cloned.1.call-start = ((), (), s32[]{:S(2)}) async-start(), calls=%async_computation.1 | async-start | bytes 2408448 | tf_op jit(solution)/shard_map/all_gather | solution.py:345
  8.8 194.8 %all-gather.10.cloned.1.call-start = ((), (), s32[]{:S(2)}) async-start(), calls=%async_computation.2 | async-start | bytes 13074432 | tf_op jit(solution)/shard_map/all_gather | solution.py:403
  9.5 202.0 %all-gather.12.cloned.1.call-start = ((), (), s32[]{:S(2)}) async-start(), calls=%async_computation.3 | async-start | bytes 13074432 | tf_op jit(solution)/shard_map/all_gather | solution.py:404
  10.1 209.7 %all-gather.14.cloned.1.call-start = ((), (), s32[]{:S(2)}) async-start(), calls=%async_computation.4 | async-start | bytes 13074432 | tf_op jit(solution)/shard_map/all_gather | solution.py:405
  13.2 54.2 %copy-start.21 = (bf16[896,128]{1,0:T(8,128)(2,1)}, bf16[896,128]{1,0:T(8,128)(2,1)S(1)}, u32[]{:S(2)}) copy-start(bf16[896,128]{1,0:T(8,128)(2,1)S(1)} %all_gather.39) | copy-start | bytes 688132
  18.8 59.7 %copy-start.32 = (f32[896]{0:T(1024)}, f32[896]{0:T(1024)S(1)}, u32[]{:S(2)}) copy-start(f32[896]{0:T(1024)S(1)} %convert_element_type.205) | copy-start | bytes 10756
  19.0 48.4 %copy-start.38 = (f32[256]{0:T(256)}, f32[256]{0:T(256)S(1)}, u32[]{:S(2)}) copy-start(f32[256]{0:T(256)S(1)} %fusion.56) | copy-start | bytes 3076
  19.0 59.5 %copy-start.34 = (f32[256]{0:T(256)}, f32[256]{0:T(256)S(1)}, u32[]{:S(2)}) copy-start(f32[256]{0:T(256)S(1)} %fusion.80) | copy-start | bytes 3076
  89.8 7.6 copy-start
  211.5 8.3 %copy-start.18 = (bf16[1,256,896]{2,1,0:T(8,128)(2,1)S(1)}, bf16[1,256,896]{2,1,0:T(8,128)(2,1)}, u32[]{:S(2)}) copy-start(bf16[1,256,896]{2,1,0:T(8,128)(2,1)} %param.22) | copy-start | bytes 1376260
  231.0 6.4 copy-start.17
  231.0 12.4 %slice-start.3 = ((s8[8716288]{0:T(1024)(128)(4,1)}), s8[4194304]{0:T(1024)(128)(4,1)S(1)}, s32[]{:S(2)}) async-start(s8[8716288]{0:T(1024)(128)(4,1)} %bitcast.300), calls=%async_computation.8 | async-start | bytes 8388608
  231.0 12.4 %slice-start.4 = ((s8[8716288]{0:T(1024)(128)(4,1)}), s8[4194304]{0:T(1024)(128)(4,1)S(1)}, s32[]{:S(2)}) async-start(s8[8716288]{0:T(1024)(128)(4,1)} %bitcast.300), calls=%async_computation.9 | async-start | bytes 8388608
  237.4 6.0 slice-start.5
  237.4 11.5 %slice-start.6 = ((s8[8716288]{0:T(1024)(128)(4,1)}), s8[4194304]{0:T(1024)(128)(4,1)S(1)}, s32[]{:S(2)}) async-start(s8[8716288]{0:T(1024)(128)(4,1)} %bitcast.302), calls=%async_computation.11 | async-start | bytes 8388608
  237.4 11.5 %slice-start.7 = ((s8[8716288]{0:T(1024)(128)(4,1)}), s8[4194304]{0:T(1024)(128)(4,1)S(1)}, s32[]{:S(2)}) async-start(s8[8716288]{0:T(1024)(128)(4,1)} %bitcast.302), calls=%async_computation.12 | async-start | bytes 8388608
  243.4 5.5 slice-start.8
  243.5 5.5 copy-start.8
  249.0 6.4 copy-start.10
  257.7 168.5 %copy-start.33 = (f32[896]{0:T(1024)S(1)}, f32[896]{0:T(1024)}, u32[]{:S(2)}) copy-start(f32[896]{0:T(1024)} %copy-done.32) | copy-start | bytes 10756
  257.7 168.5 %copy-start.35 = (f32[256]{0:T(256)S(1)}, f32[256]{0:T(256)}, u32[]{:S(2)}) copy-start(f32[256]{0:T(256)} %copy-done.34) | copy-start | bytes 3076
  260.0 5.2 copy-start.2
  265.2 7.7 copy-start.1
  282.1 7.7 copy-start.1
  293.7 5.2 copy-start.2
  299.0 7.7 copy-start.1
  315.8 7.7 copy-start.1
  332.7 7.7 copy-start.1
  349.6 7.7 copy-start.1
  366.5 7.7 copy-start.1
  378.1 5.2 copy-start.2
  383.3 7.7 copy-start.1
  392.9 35.4 %copy-start.26 = (f32[256,32]{0,1:T(8,128)S(1)}, f32[256,32]{0,1:T(8,128)}, u32[]{:S(2)}) copy-start(f32[256,32]{0,1:T(8,128)} %get-tuple-element.345) | copy-start | bytes 98308
  392.9 35.4 %copy-start.27 = (f32[256,32]{0,1:T(8,128)S(1)}, f32[256,32]{0,1:T(8,128)}, u32[]{:S(2)}) copy-start(f32[256,32]{0,1:T(8,128)} %get-tuple-element.347) | copy-start | bytes 98308
  396.9 37.2 %copy-start.24 = (bf16[896,128]{1,0:T(8,128)(2,1)S(1)}, bf16[896,128]{1,0:T(8,128)(2,1)}, u32[]{:S(2)}) copy-start(bf16[896,128]{1,0:T(8,128)(2,1)} %copy-done.23) | copy-start | bytes 688132
  396.9 37.5 %copy-start.22 = (bf16[896,128]{1,0:T(8,128)(2,1)S(1)}, bf16[896,128]{1,0:T(8,128)(2,1)}, u32[]{:S(2)}) copy-start(bf16[896,128]{1,0:T(8,128)(2,1)} %copy-done.21) | copy-start | bytes 688132
  425.3 9.1 %copy-start.25 = (bf16[256,256]{1,0:T(8,128)(2,1)S(1)}, bf16[256,256]{1,0:T(8,128)(2,1)}, u32[]{:S(2)}) copy-start(bf16[256,256]{1,0:T(8,128)(2,1)} %shard_map.273) | copy-start | bytes 393220
  428.2 7.5 copy-start.20
  428.3 7.4 copy-start.14
  441.0 22.6 %slice-start = ((s8[8716288]{0:T(1024)(128)(4,1)}), s8[327680]{0:T(1024)(128)(4,1)S(1)}, s32[]{:S(2)}) async-start(s8[8716288]{0:T(1024)(128)(4,1)} %bitcast.283), calls=%async_computation.5 | async-start | bytes 655360
  441.0 22.6 %slice-start.1 = ((s8[8716288]{0:T(1024)(128)(4,1)}), s8[4194304]{0:T(1024)(128)(4,1)S(1)}, s32[]{:S(2)}) async-start(s8[8716288]{0:T(1024)(128)(4,1)} %bitcast.283), calls=%async_computation.6 | async-start | bytes 8388608
  452.6 11.1 %slice-start.2 = ((s8[8716288]{0:T(1024)(128)(4,1)}), s8[4194304]{0:T(1024)(128)(4,1)S(1)}, s32[]{:S(2)}) async-start(s8[8716288]{0:T(1024)(128)(4,1)} %bitcast.283), calls=%async_computation.7 | async-start | bytes 8388608
  463.7 6.7 copy-start.28
  465.1 6.6 copy-start.12
  466.5 6.5 copy-start.11
  467.8 6.6 copy-start.29
  767.6 10.1 %copy-start.39 = (f32[256]{0:T(256)S(1)}, f32[256]{0:T(256)}, u32[]{:S(2)}) copy-start(f32[256]{0:T(256)} %copy-done.38) | copy-start | bytes 3076
  767.6 15.2 %slice-start.9 = ((s8[4358144]{0:T(1024)(128)(4,1)}), s8[163840]{0:T(1024)(128)(4,1)S(1)}, s32[]{:S(2)}) async-start(s8[4358144]{0:T(1024)(128)(4,1)} %bitcast.307), calls=%async_computation.14 | async-start | bytes 327680
  769.3 13.5 %slice-start.11 = ((s8[4358144]{0:T(1024)(128)(4,1)}), s8[4194304]{0:T(1024)(128)(4,1)S(1)}, s32[]{:S(2)}) async-start(s8[4358144]{0:T(1024)(128)(4,1)} %bitcast.309), calls=%async_computation.16 | async-start | bytes 8388608
  771.3 11.5 %slice-start.10 = ((s8[4358144]{0:T(1024)(128)(4,1)}), s8[4194304]{0:T(1024)(128)(4,1)S(1)}, s32[]{:S(2)}) async-start(s8[4358144]{0:T(1024)(128)(4,1)} %bitcast.307), calls=%async_computation.15 | async-start | bytes 8388608
  771.3 11.5 %slice-start.12 = ((s8[4358144]{0:T(1024)(128)(4,1)}), s8[163840]{0:T(1024)(128)(4,1)S(1)}, s32[]{:S(2)}) async-start(s8[4358144]{0:T(1024)(128)(4,1)} %bitcast.309), calls=%async_computation.17 | async-start | bytes 327680
  792.9 10.6 %slice-start.13 = ((s8[8716288]{0:T(1024)(128)(4,1)}), s8[327680]{0:T(1024)(128)(4,1)S(1)}, s32[]{:S(2)}) async-start(s8[8716288]{0:T(1024)(128)(4,1)} %bitcast.337), calls=%async_computation.18 | async-start | bytes 655360
  792.9 10.6 %slice-start.14 = ((s8[8716288]{0:T(1024)(128)(4,1)}), s8[4194304]{0:T(1024)(128)(4,1)S(1)}, s32[]{:S(2)}) async-start(s8[8716288]{0:T(1024)(128)(4,1)} %bitcast.337), calls=%async_computation.19 | async-start | bytes 8388608
  797.3 6.2 copy-start.9
  797.3 6.2 copy-start.15
  797.3 7.2 slice-start.15
  (26 other events, 115.3 us)
Sparse Core Ops, SparseCore 0:
  9.6 12.7 all-gather.5
  23.9 10.8 all-gather.7
  36.4 22.1 all-gather.9
  60.0 22.1 all-gather.11
  83.6 22.1 all-gather.13
